TPU v7x, 32 devices: a whole 2x2x4 slice. The times are simulated.
32 devices in a mesh: radius: 2 (over core), polar: 4 (over y, x), group: 4 (over z).
Axes of the slice: x: 2, y: 2, z: 4, core: 2. Of those that a mesh axis runs over, the one named last changes fastest.
Arguments:
- density: float32 [96, 1024], P('radius', 'polar'), may hold values from 0.3 to 3
- opacity: bfloat16 [64, 96, 1024], P('group', 'radius', 'polar'), may hold values from 0.049804688 to 5
- radiation_old: float32 [64, 96, 1024], P('group', 'radius', 'polar'), may hold values from 0.5 to 2
- material_old: float32 [96, 1024], P('radius', 'polar'), may hold values from 0.5 to 2
- weights: float32 [64], P('group'), may hold values from 0.5 to 2
- stellar_flux: float32 [96], P('radius'), may hold values from 10 to 100
Outputs:
- energy: float32 [64, 96, 1024], P('group', 'radius', 'polar')
- material_now: float32 [96, 1024], P('radius', 'polar')
- column: float32 [96, 1024], P('radius', 'polar')
All inputs are finite; a program needn't handle non-finite values.
Results may differ from a plain program's by a relative error of at most 0.0003.
Values sent between devices are 32-bit elements; how exact they have to be, the bound alone decides.
A program may use at most 64 MiB of HBM per device.

v0:
```python
import jax
import jax.numpy as jnp
from jax import lax
from jax.sharding import PartitionSpec as P

ITERS = 3


def padded_2(cells, sides, width):
    for axis, dim in sides:
        count = lax.axis_size(axis)
        ends = count - 1
        head = lax.slice_in_dim(cells, 0, width, axis=dim)
        tail = lax.slice_in_dim(cells, cells.shape[dim] - width, cells.shape[dim], axis=dim)
        cells = jnp.concatenate(
            [
                lax.ppermute(tail, axis, [(i, (i + 1) % count) for i in range(ends)]),
                cells,
                lax.ppermute(head, axis, [((i + 1) % count, i) for i in range(ends)]),
            ],
            axis=dim,
        )
    return cells


def prefix(part, axis, combine, identity):
    place = lax.axis_index(axis)
    gathered = lax.all_gather(part, axis)
    state = jnp.zeros_like(part) + jnp.asarray(identity, part.dtype)

    def one(turn, state):
        return combine(state, lax.dynamic_index_in_dim(gathered, turn, 0, False))

    return lax.fori_loop(0, place, one, state)


def harmonic(lower_value, upper_value):
    return 2.0 * lower_value * upper_value / (lower_value + upper_value)


def harmonic_safe(lower_value, upper_value):
    total = lower_value + upper_value
    return 2.0 * lower_value * upper_value / jnp.where(total > 0.0, total, 1.0)


def add_pair(earlier, following):
    return earlier + following


def apply_padded(padded, field, absorb, face_coeffs):
    return (
        (1.0 + absorb) * field
        + face_coeffs[0] * (field - padded[:, 2:, 1:-1])
        + face_coeffs[1] * (field - padded[:, :-2, 1:-1])
        + face_coeffs[2] * (field - padded[:, 1:-1, 2:])
        + face_coeffs[3] * (field - padded[:, 1:-1, :-2])
    )


def local_dot(left_field, right_field):
    return jnp.sum(left_field * right_field, axis=(1, 2))


def wide_operator(absorb, diffusion):
    group_count = absorb.shape[0]
    stacked = jnp.concatenate([absorb, diffusion], axis=0)
    extended = padded_2(stacked, (("radius", 1), ("polar", 2)), 2)
    absorb_mid = extended[:group_count, 1:-1, 1:-1]
    spread = extended[group_count:]
    center = spread[:, 1:-1, 1:-1]
    faces_mid = (
        harmonic_safe(center, spread[:, 2:, 1:-1]),
        harmonic_safe(spread[:, :-2, 1:-1], center),
        harmonic_safe(center, spread[:, 1:-1, 2:]),
        harmonic_safe(spread[:, 1:-1, :-2], center),
    )
    return (absorb_mid, faces_mid)


def solve_blocked(energy, residual, absorb, face_coeffs, absorb_mid, faces_mid):
    band = padded_2(residual, (("radius", 1), ("polar", 2)), 2)
    applied_mid = apply_padded(band, band[:, 1:-1, 1:-1], absorb_mid, faces_mid)
    applied = applied_mid[:, 1:-1, 1:-1]
    twice = apply_padded(applied_mid, applied, absorb, face_coeffs)
    gram_entries = lax.psum(
        jnp.stack(
            [
                local_dot(residual, residual),
                local_dot(residual, applied),
                local_dot(applied, applied),
                local_dot(residual, twice),
                local_dot(applied, twice),
            ]
        ),
        ("radius", "polar"),
    )
    norm_first = gram_entries[0]
    first_curv = gram_entries[1]
    image_norm = gram_entries[2]
    cross_twice = gram_entries[3]
    image_twice = gram_entries[4]
    step_first = norm_first / first_curv
    norm_second = norm_first - 2.0 * step_first * first_curv + step_first * step_first * image_norm
    ratio_value = norm_second / norm_first
    scaled = 1.0 + ratio_value
    second_curv = (
        scaled * scaled * first_curv
        - scaled * step_first * (cross_twice + image_norm)
        + step_first * step_first * image_twice
    )
    step_second = norm_second / second_curv
    coef_res = (step_first + step_second * scaled)[:, None, None]
    coef_img = (step_second * step_first)[:, None, None]
    energy = energy + coef_res * residual - coef_img * applied
    residual = (
        residual - (step_first + step_second * scaled)[:, None, None] * applied + coef_img * twice
    )
    return (energy, residual)


def per_device(density, opacity, radiation_old, material_old, weights, stellar_flux):
    polar_cells = density.shape[1]
    polar_total = polar_cells * lax.axis_size("polar")
    row_sums = jnp.sum(density, axis=1)
    carried = prefix(row_sums, "polar", add_pair, jnp.zeros_like(row_sums))
    upper_tri = (
        lax.broadcasted_iota(jnp.int32, (polar_cells, polar_cells), 0)
        <= lax.broadcasted_iota(jnp.int32, (polar_cells, polar_cells), 1)
    ).astype(jnp.float32)
    within = jnp.dot(
        density, upper_tri, precision=lax.Precision.HIGHEST, preferred_element_type=jnp.float32
    )
    column = 2.0 / polar_total * (carried[:, None] + within)
    heating = stellar_flux[:, None] * density * jnp.exp(-column)
    absorb = opacity.astype(jnp.float32) * density[None]
    group_weight = weights[:, None, None]
    old_padded = padded_2(radiation_old, (("radius", 1), ("polar", 2)), 1)
    radial_slope = 0.5 * (old_padded[:, 2:, 1:-1] - old_padded[:, :-2, 1:-1])
    polar_slope = 0.5 * (old_padded[:, 1:-1, 2:] - old_padded[:, 1:-1, :-2])
    ratio_value = jnp.sqrt(radial_slope * radial_slope + polar_slope * polar_slope) / (
        absorb * radiation_old
    )
    limiter = (2.0 + ratio_value) / (6.0 + 3.0 * ratio_value + ratio_value * ratio_value)
    diffusion = limiter / absorb
    coeff_padded = padded_2(diffusion, (("radius", 1), ("polar", 2)), 1)
    face_coeffs = (
        harmonic(diffusion, coeff_padded[:, 2:, 1:-1]),
        harmonic(coeff_padded[:, :-2, 1:-1], diffusion),
        harmonic(diffusion, coeff_padded[:, 1:-1, 2:]),
        harmonic(coeff_padded[:, 1:-1, :-2], diffusion),
    )
    residual = (
        absorb * group_weight * material_old[None]
        + radiation_old
        - apply_padded(old_padded, radiation_old, absorb, face_coeffs)
    )
    energy = radiation_old
    absorb_mid, faces_mid = wide_operator(absorb, diffusion)
    emission_local = jnp.sum(absorb * group_weight, axis=0)
    fixed_terms = 16.0 * density * material_old + heating
    capacity = 16.0 * density + lax.psum(emission_local, "group")
    material_now = material_old
    for round_index in range(ITERS):
        energy, residual = solve_blocked(
            energy, residual, absorb, face_coeffs, absorb_mid, faces_mid
        )
        absorbed_local = jnp.sum(absorb * energy, axis=0)
        material_next = (fixed_terms + lax.psum(absorbed_local, "group")) / capacity
        if round_index + 1 < ITERS:
            residual = residual + absorb * group_weight * (material_next - material_now)[None]
        material_now = material_next
    return (energy, material_now, column)


def solution(mesh):
    return jax.shard_map(
        per_device,
        mesh=mesh,
        in_specs=(
            P("radius", "polar"),
            P("group", "radius", "polar"),
            P("group", "radius", "polar"),
            P("radius", "polar"),
            P("group"),
            P("radius"),
        ),
        out_specs=(P("group", "radius", "polar"), P("radius", "polar"), P("radius", "polar")),
        check_vma=False,
    )
```

profile of v0, /device:TPU:0, one launch (start us, length us, event | category | flops | bytes accessed | tf_op | source)
XLA Modules:
  0.0 338.9 jit_solution(8984882082300642552)
XLA Ops:
  8.9 2.4 collective-permute-start.1
  15.8 4.9 %collective-permute-start.3 = (f32[16,50,1]{2,0,1:T(8,128)S(1)}, f32[16,50,1]{2,0,1:T(8,128)S(1)}, u32[]{:S(2)}, u32[]{:S(2)}) collective-permute-start(f32[16,50,1]{2,0,1:T(8,128)S(1)} %get-tuple-element.99), channel_id=1, source_target_pairs={{0,4},{4,8},{8,12},{1,5},{5,9},{9,13},{2,6},{6,10},{10,14},{3,7},{... | collective-permute-start | bytes 9608 | tf_op jit(solution)/shard_map/ppermute | solution.py:17
  20.7 8.3 %collective-permute-done.2 = f32[16,50,1]{2,0,1:T(8,128)S(1)} collective-permute-done((f32[16,50,1]{2,0,1:T(8,128)S(1)}, f32[16,50,1]{2,0,1:T(8,128)S(1)}, u32[]{:S(2)}, u32[]{:S(2)}) %collective-permute-start.2) | collective-permute-done | bytes 3232 | tf_op jit(solution)/shard_map/ppermute | solution.py:19
  32.0 3.0 collective-permute-start.5
  38.2 10.4 %collective-permute-start.7 = (f32[16,50,1]{2,0,1:T(8,128)S(1)}, f32[16,50,1]{2,0,1:T(8,128)}, u32[]{:S(2)}, u32[]{:S(2)}) collective-permute-start(f32[16,50,1]{2,0,1:T(8,128)S(1)} %get-tuple-element.97), channel_id=1, source_target_pairs={{0,4},{4,8},{8,12},{1,5},{5,9},{9,13},{2,6},{6,10},{10,14},{3,7},{... | collective-permute-start | bytes 9608 | tf_op jit(solution)/shard_map/ppermute | solution.py:17
  50.2 19.8 %all-reduce = f32[192]{0:T(256)S(1)} all-reduce(f32[192]{0:T(256)S(1)} %dynamic-update-slice), channel_id=2, replica_groups=mesh['radius'=2,'polar'=4,'group'=4] {'polar'}, use_global_device_ids=true, to_apply=%add | all-reduce | flops 192 | bytes 1536
  70.8 5.0 %fusion.73 = f32[16,48,256]{2,0,1:T(8,128)S(1)} fusion(f32[16,48,256]{2,0,1:T(8,128)} %copy-done.23, f32[16,1,256]{2,0,1:T(8,128)S(1)} %collective-permute-done.1, f32[16,1,256]{2,0,1:T(8,128)S(1)} %collective-permute-done, f32[16,50,1]{2,0,1:T(8,128)} %copy-done.32, f32[16,50,256]{2,0,1:T(8,128)} %copy-done.22, f32[16,50,1]{2,0,1:T(8,128)} %copy-done.33, ...), kind=kLoop, calls=%fused_computation.144 | loop fusion | flops 9240576 | bytes 3748416 | tf_op jit(solution)/shard_map/sub | solution.py:153
  78.5 3.0 collective-permute-start.8
  90.1 5.7 %collective-permute-start.10 = (f32[32,52,2]{1,0,2:T(8,128)S(1)}, f32[32,52,2]{1,0,2:T(8,128)S(1)}, u32[]{:S(2)}, u32[]{:S(2)}) collective-permute-start(f32[32,52,2]{1,0,2:T(8,128)S(1)} %copy.75), channel_id=1, source_target_pairs={{0,4},{4,8},{8,12},{1,5},{5,9},{9,13},{2,6},{6,10},{10,14},{3,7},{... | collective-permute-start | bytes 39944 | tf_op jit(solution)/shard_map/ppermute | solution.py:17
  97.8 10.9 %collective-permute-done.15 = f32[16,52,2]{2,0,1:T(8,128)} collective-permute-done((f32[16,52,2]{2,0,1:T(8,128)}, f32[16,52,2]{2,0,1:T(8,128)}, u32[]{:S(2)}, u32[]{:S(2)}) %collective-permute-start.15) | collective-permute-done | bytes 6688 | tf_op jit(solution)/shard_map/ppermute | solution.py:19
  108.8 2.6 pad_maximum_fusion.2
  114.7 2.7 pad_maximum_fusion
  117.8 5.8 %fusion.26 = (f32[16,50,258]{2,0,1:T(8,128)S(1)}, f32[16,50,258]{2,0,1:T(8,128)}, f32[16,50,258]{2,0,1:T(8,128)}) fusion(f32[16,52,2]{2,0,1:T(8,128)S(1)} %copy-done.31, f32[16,2,256]{2,0,1:T(8,128)S(1)} %copy-done.37, f32[16,48,256]{2,0,1:T(8,128)S(1)} %copy-done.1, f32[16,2,256]{2,0,1:T(8,128)S(1)} %copy-done.35, f32[16,52,2]{2,0,1:T(8,128)} %collective-permute-done.15, ...), kind=kLoop, calls=%fused_computation.53 | loop fusion | flops 10526400 | bytes 10851840 | tf_op jit(solution)/shard_map/add | solution.py:52
  123.6 4.7 %multiply_reduce_fusion.13 = (f32[16]{0:T(128)S(1)}, f32[16]{0:T(128)S(1)}, f32[16]{0:T(128)S(1)}, f32[16]{0:T(128)S(1)}, f32[16]{0:T(128)S(1)}, /*index=5*/f32[16,48,256]{2,0,1:T(8,128)}) fusion(f32[16,50,258]{2,0,1:T(8,128)S(1)} %get-tuple-element.84, f32[16,48,256]{2,0,1:T(8,128)S(1)} %copy-done.1, f32[16,48,256]{2,0,1:T(8,128)S(1)} %get-tuple-element.112, ...), kind=kLoop, calls=%fused_computation.172 | loop fusion | flops 9633712 | bytes 6773312 | tf_op jit(solution)/shard_map/reduce_sum | solution.py:61
  128.4 12.6 %psum.49 = f32[5,16]{1,0:T(8,128)S(1)} all-reduce(f32[5,16]{1,0:T(8,128)S(1)} %stack.59), channel_id=1, replica_groups=mesh['radius'=2,'polar'=4,'group'=4] {'radius','polar'}, use_global_device_ids=true, to_apply=%region_5.6 | all-reduce | flops 80 | bytes 640 | tf_op jit(solution)/shard_map/psum | solution.py:85
  141.1 4.3 %fusion.84 = (f32[48,256]{1,0:T(8,128)}, f32[48,256]{1,0:T(8,128)}, f32[16,48,256]{2,0,1:T(8,128)}) fusion(f32[16]{0:T(128)S(1)} %copy-done.43, f32[48,256]{1,0:T(8,128)S(1)} %copy-done.19, bf16[16,48,256]{2,1,0:T(8,128)(2,1)} %param.9, f32[16,50,258]{2,0,1:T(8,128)} %copy-done.8, f32[16]{0:T(128)S(1)} %mul.755, f32[16,48,256]{2,0,1:T(8,128)} %copy-done, ...), kind=kLoop, calls=%fused_computation.183 | loop fusion | flops 1941504 | bytes 3686592 | tf_op jit(solution)/shard_map/reduce_sum | solution.py:159
  145.4 36.5 %all-reduce.4.cloned.1.call-done = (f32[48,256]{1,0:T(8,128)}, f32[48,256]{1,0:T(8,128)}) async-done(((f32[48,256]{1,0:T(8,128)}, f32[48,256]{1,0:T(8,128)}), (f32[48,256]{1,0:T(8,128)}, f32[48,256]{1,0:T(8,128)})) %all-reduce.4.cloned.1.call-update) | async-done | bytes 98320 | tf_op jit(solution)/shard_map/psum | solution.py:168
  190.5 3.4 collective-permute-start.18
  195.3 7.9 %collective-permute-done.18 = f32[16,52,2]{2,0,1:T(8,128)S(1)} collective-permute-done((f32[16,52,2]{2,0,1:T(8,128)S(1)}, f32[16,52,2]{2,0,1:T(8,128)S(1)}, u32[]{:S(2)}, u32[]{:S(2)}) %collective-permute-start.18) | collective-permute-done | bytes 6688 | tf_op jit(solution)/shard_map/ppermute | solution.py:17
  203.2 11.1 %collective-permute-done.19 = f32[16,52,2]{2,0,1:T(8,128)S(1)} collective-permute-done((f32[16,52,2]{2,0,1:T(8,128)S(1)}, f32[16,52,2]{2,0,1:T(8,128)S(1)}, u32[]{:S(2)}, u32[]{:S(2)}) %collective-permute-start.19) | collective-permute-done | bytes 6688 | tf_op jit(solution)/shard_map/ppermute | solution.py:19
  214.8 3.0 fusion.16
  217.8 4.7 %multiply_reduce_fusion.7 = (f32[16]{0:T(128)S(1)}, f32[16]{0:T(128)S(1)}, f32[16]{0:T(128)S(1)}, f32[16]{0:T(128)S(1)}, f32[16]{0:T(128)S(1)}, /*index=5*/f32[16,48,256]{2,0,1:T(8,128)}) fusion(f32[16,50,258]{2,0,1:T(8,128)S(1)} %fusion.16, f32[16,48,256]{2,0,1:T(8,128)S(1)} %multiply_add_fusion.1, f32[16,48,256]{2,0,1:T(8,128)S(1)} %get-tuple-element.112, ...), kind=kLoop, calls=%fused_computation.164 | loop fusion | flops 9633712 | bytes 6773312 | tf_op jit(solution)/shard_map/reduce_sum | solution.py:61
  222.5 14.5 %psum.52 = f32[5,16]{1,0:T(8,128)S(1)} all-reduce(f32[5,16]{1,0:T(8,128)S(1)} %stack.65), channel_id=1, replica_groups=mesh['radius'=2,'polar'=4,'group'=4] {'radius','polar'}, use_global_device_ids=true, to_apply=%region_18.19 | all-reduce | flops 80 | bytes 640 | tf_op jit(solution)/shard_map/psum | solution.py:85
  237.1 3.2 multiply_reduce_fusion.6
  240.3 18.2 %psum.53 = f32[48,256]{1,0:T(8,128)S(1)} all-reduce(f32[48,256]{1,0:T(8,128)S(1)} %get-tuple-element.69), channel_id=1, replica_groups=mesh['radius'=2,'polar'=4,'group'=4] {'group'}, use_global_device_ids=true, to_apply=%region_20.21 | all-reduce | flops 12288 | bytes 98304 | tf_op jit(solution)/shard_map/psum | solution.py:168
  266.2 2.5 collective-permute-start.22
  270.2 7.9 %collective-permute-done.22 = f32[16,52,2]{2,0,1:T(8,128)S(1)} collective-permute-done((f32[16,52,2]{2,0,1:T(8,128)S(1)}, f32[16,52,2]{2,0,1:T(8,128)S(1)}, u32[]{:S(2)}, u32[]{:S(2)}) %collective-permute-start.22) | collective-permute-done | bytes 6688 | tf_op jit(solution)/shard_map/ppermute | solution.py:17
  278.1 12.8 %collective-permute-done.23 = f32[16,52,2]{2,0,1:T(8,128)S(1)} collective-permute-done((f32[16,52,2]{2,0,1:T(8,128)S(1)}, f32[16,52,2]{2,0,1:T(8,128)S(1)}, u32[]{:S(2)}, u32[]{:S(2)}) %collective-permute-start.23) | collective-permute-done | bytes 6688 | tf_op jit(solution)/shard_map/ppermute | solution.py:19
  291.4 3.0 fusion.6
  294.5 4.1 %multiply_reduce_fusion.1 = (f32[16]{0:T(128)S(1)}, f32[16]{0:T(128)S(1)}, f32[16]{0:T(128)S(1)}, f32[16]{0:T(128)S(1)}, f32[16]{0:T(128)S(1)}) fusion(f32[16,50,258]{2,0,1:T(8,128)S(1)} %fusion.6, f32[16,48,256]{2,0,1:T(8,128)S(1)} %multiply_add_fusion, f32[16,48,256]{2,0,1:T(8,128)S(1)} %get-tuple-element.112, ...), kind=kLoop, calls=%fused_computation.156 | loop fusion | flops 9633712 | bytes 5986880 | tf_op jit(solution)/shard_map/reduce_sum | solution.py:61
  298.5 13.1 %psum.54 = f32[5,16]{1,0:T(8,128)S(1)} all-reduce(f32[5,16]{1,0:T(8,128)S(1)} %stack.71), channel_id=1, replica_groups=mesh['radius'=2,'polar'=4,'group'=4] {'radius','polar'}, use_global_device_ids=true, to_apply=%region_26.27 | all-reduce | flops 80 | bytes 640 | tf_op jit(solution)/shard_map/psum | solution.py:85
  313.7 16.4 %psum.55 = f32[48,256]{1,0:T(8,128)S(1)} all-reduce(f32[48,256]{1,0:T(8,128)S(1)} %get-tuple-element.63), channel_id=1, replica_groups=mesh['radius'=2,'polar'=4,'group'=4] {'group'}, use_global_device_ids=true, to_apply=%region_28.29 | all-reduce | flops 12288 | bytes 98304 | tf_op jit(solution)/shard_map/psum | solution.py:168
  (184 shorter events, 54.9 us)
Async XLA Ops:
  7.2 174.7 %all-reduce.4.cloned.1.call-start = ((), (), s32[]{:S(2)}) async-start(), calls=%async_computation | async-start | bytes 196608 | tf_op jit(solution)/shard_map/psum | solution.py:168
  8.9 3.7 %collective-permute-start.1 = (f32[16,1,256]{2,0,1:T(8,128)S(1)}, f32[16,1,256]{2,0,1:T(8,128)S(1)}, u32[]{:S(2)}, u32[]{:S(2)}) collective-permute-start(f32[16,1,256]{2,0,1:T(8,128)S(1)} %get-tuple-element.110), channel_id=1, source_target_pairs={{0,16},{1,17},{2,18},{3,19},{4,20},{5,21},{6,22},{7,23},{8,24},{9,... | collective-permute-start | bytes 49160 | tf_op jit(solution)/shard_map/ppermute | solution.py:17
  11.3 3.1 collective-permute-start
  14.5 14.5 %collective-permute-start.2 = (f32[16,50,1]{2,0,1:T(8,128)S(1)}, f32[16,50,1]{2,0,1:T(8,128)S(1)}, u32[]{:S(2)}, u32[]{:S(2)}) collective-permute-start(f32[16,50,1]{2,0,1:T(8,128)S(1)} %get-tuple-element.100), channel_id=1, source_target_pairs={{4,0},{8,4},{12,8},{5,1},{9,5},{13,9},{6,2},{10,6},{14,10},{7,3},{... | collective-permute-start | bytes 9608 | tf_op jit(solution)/shard_map/ppermute | solution.py:19
  15.8 13.9 %collective-permute-start.3 = (f32[16,50,1]{2,0,1:T(8,128)S(1)}, f32[16,50,1]{2,0,1:T(8,128)S(1)}, u32[]{:S(2)}, u32[]{:S(2)}) collective-permute-start(f32[16,50,1]{2,0,1:T(8,128)S(1)} %get-tuple-element.99), channel_id=1, source_target_pairs={{0,4},{4,8},{8,12},{1,5},{5,9},{9,13},{2,6},{6,10},{10,14},{3,7},{... | collective-permute-start | bytes 9608 | tf_op jit(solution)/shard_map/ppermute | solution.py:17
  30.7 56.3 %copy-start.12 = (f32[16,48,256]{2,0,1:T(8,128)}, f32[16,48,256]{2,0,1:T(8,128)S(1)}, u32[]{:S(2)}) copy-start(f32[16,48,256]{2,0,1:T(8,128)S(1)} %get-tuple-element.111) | copy-start | bytes 2359300
  30.7 4.3 %collective-permute-start.4 = (f32[16,1,256]{2,0,1:T(8,128)S(1)}, f32[16,1,256]{2,0,1:T(8,128)S(1)}, u32[]{:S(2)}, u32[]{:S(2)}) collective-permute-start(f32[16,1,256]{2,0,1:T(8,128)S(1)} %get-tuple-element.108), channel_id=1, source_target_pairs={{16,0},{17,1},{18,2},{19,3},{20,4},{21,5},{22,6},{23,7},{24,8},{25... | collective-permute-start | bytes 49160 | tf_op jit(solution)/shard_map/ppermute | solution.py:19
  32.0 3.9 %collective-permute-start.5 = (f32[16,1,256]{2,0,1:T(8,128)S(1)}, f32[16,1,256]{2,0,1:T(8,128)S(1)}, u32[]{:S(2)}, u32[]{:S(2)}) collective-permute-start(f32[16,1,256]{2,0,1:T(8,128)S(1)} %get-tuple-element.107), channel_id=1, source_target_pairs={{0,16},{1,17},{2,18},{3,19},{4,20},{5,21},{6,22},{7,23},{8,24},{9,... | collective-permute-start | bytes 49160 | tf_op jit(solution)/shard_map/ppermute | solution.py:17
  36.0 34.8 %copy-start.40 = (f32[48,256]{1,0:T(8,128)S(1)}, f32[48,256]{1,0:T(8,128)}, u32[]{:S(2)}) copy-start(f32[48,256]{1,0:T(8,128)} %param.11) | copy-start | bytes 147460
  36.0 34.8 %copy-start.42 = (f32[16]{0:T(128)S(1)}, f32[16]{0:T(128)}, u32[]{:S(2)}) copy-start(f32[16]{0:T(128)} %param.12) | copy-start | bytes 196
  36.9 33.9 %collective-permute-start.6 = (f32[16,50,1]{2,0,1:T(8,128)}, f32[16,50,1]{2,0,1:T(8,128)S(1)}, u32[]{:S(2)}, u32[]{:S(2)}) collective-permute-start(f32[16,50,1]{2,0,1:T(8,128)} %get-tuple-element.98), channel_id=1, source_target_pairs={{4,0},{8,4},{12,8},{5,1},{9,5},{13,9},{6,2},{10,6},{14,10},{7,3},{... | collective-permute-start | bytes 9608 | tf_op jit(solution)/shard_map/ppermute | solution.py:19
  38.2 32.6 %collective-permute-start.7 = (f32[16,50,1]{2,0,1:T(8,128)S(1)}, f32[16,50,1]{2,0,1:T(8,128)}, u32[]{:S(2)}, u32[]{:S(2)}) collective-permute-start(f32[16,50,1]{2,0,1:T(8,128)S(1)} %get-tuple-element.97), channel_id=1, source_target_pairs={{0,4},{4,8},{8,12},{1,5},{5,9},{9,13},{2,6},{6,10},{10,14},{3,7},{... | collective-permute-start | bytes 9608 | tf_op jit(solution)/shard_map/ppermute | solution.py:17
  75.8 32.9 %copy-start = (f32[16,48,256]{2,0,1:T(8,128)}, f32[16,48,256]{2,0,1:T(8,128)S(1)}, u32[]{:S(2)}) copy-start(f32[16,48,256]{2,0,1:T(8,128)S(1)} %fusion.73) | copy-start | bytes 2359300
  75.9 7.0 %collective-permute-start.12 = (f32[16,2,256]{2,0,1:T(8,128)S(1)}, f32[16,2,256]{2,0,1:T(8,128)S(1)}, u32[]{:S(2)}, u32[]{:S(2)}) collective-permute-start(f32[16,2,256]{2,0,1:T(8,128)S(1)} %get-tuple-element.105), channel_id=1, source_target_pairs={{0,16},{1,17},{2,18},{3,19},{4,20},{5,21},{6,22},{7,23},{8,24},{9,... | collective-permute-start | bytes 98312 | tf_op jit(solution)/shard_map/ppermute | solution.py:17
  77.2 5.7 %collective-permute-start.13 = (f32[16,2,256]{2,0,1:T(8,128)S(1)}, f32[16,2,256]{2,0,1:T(8,128)S(1)}, u32[]{:S(2)}, u32[]{:S(2)}) collective-permute-start(f32[16,2,256]{2,0,1:T(8,128)S(1)} %get-tuple-element.106), channel_id=1, source_target_pairs={{16,0},{17,1},{18,2},{19,3},{20,4},{21,5},{22,6},{23,7},{24,8},{25... | collective-permute-start | bytes 98312 | tf_op jit(solution)/shard_map/ppermute | solution.py:19
  78.5 8.5 %collective-permute-start.8 = (f32[32,2,256]{2,0,1:T(8,128)S(1)}, f32[32,2,256]{2,0,1:T(8,128)S(1)}, u32[]{:S(2)}, u32[]{:S(2)}) collective-permute-start(f32[32,2,256]{2,0,1:T(8,128)S(1)} %get-tuple-element.89), channel_id=1, source_target_pairs={{0,16},{1,17},{2,18},{3,19},{4,20},{5,21},{6,22},{7,23},{8,24},{9,... | collective-permute-start | bytes 196616 | tf_op jit(solution)/shard_map/ppermute | solution.py:17
  81.5 5.5 %collective-permute-start.9 = (f32[32,2,256]{2,0,1:T(8,128)S(1)}, f32[32,2,256]{2,0,1:T(8,128)S(1)}, u32[]{:S(2)}, u32[]{:S(2)}) collective-permute-start(f32[32,2,256]{2,0,1:T(8,128)S(1)} %get-tuple-element.90), channel_id=1, source_target_pairs={{16,0},{17,1},{18,2},{19,3},{20,4},{21,5},{22,6},{23,7},{24,8},{25... | collective-permute-start | bytes 196616 | tf_op jit(solution)/shard_map/ppermute | solution.py:19
  84.0 13.8 %collective-permute-start.14 = (f32[16,52,2]{2,0,1:T(8,128)}, f32[16,52,2]{2,0,1:T(8,128)S(1)}, u32[]{:S(2)}, u32[]{:S(2)}) collective-permute-start(f32[16,52,2]{2,0,1:T(8,128)} %get-tuple-element.96), channel_id=1, source_target_pairs={{0,4},{4,8},{8,12},{1,5},{5,9},{9,13},{2,6},{6,10},{10,14},{3,7},{... | collective-permute-start | bytes 19976 | tf_op jit(solution)/shard_map/ppermute | solution.py:17
  85.7 23.1 %collective-permute-start.15 = (f32[16,52,2]{2,0,1:T(8,128)}, f32[16,52,2]{2,0,1:T(8,128)}, u32[]{:S(2)}, u32[]{:S(2)}) collective-permute-start(f32[16,52,2]{2,0,1:T(8,128)} %get-tuple-element.95), channel_id=1, source_target_pairs={{4,0},{8,4},{12,8},{5,1},{9,5},{13,9},{6,2},{10,6},{14,10},{7,3},{... | collective-permute-start | bytes 19976 | tf_op jit(solution)/shard_map/ppermute | solution.py:19
  90.1 21.3 %collective-permute-start.10 = (f32[32,52,2]{1,0,2:T(8,128)S(1)}, f32[32,52,2]{1,0,2:T(8,128)S(1)}, u32[]{:S(2)}, u32[]{:S(2)}) collective-permute-start(f32[32,52,2]{1,0,2:T(8,128)S(1)} %copy.75), channel_id=1, source_target_pairs={{0,4},{4,8},{8,12},{1,5},{5,9},{9,13},{2,6},{6,10},{10,14},{3,7},{... | collective-permute-start | bytes 39944 | tf_op jit(solution)/shard_map/ppermute | solution.py:17
  96.3 16.7 %collective-permute-start.11 = (f32[32,52,2]{1,0,2:T(8,128)S(1)}, f32[32,52,2]{1,0,2:T(8,128)S(1)}, u32[]{:S(2)}, u32[]{:S(2)}) collective-permute-start(f32[32,52,2]{1,0,2:T(8,128)S(1)} %copy.76), channel_id=1, source_target_pairs={{4,0},{8,4},{12,8},{5,1},{9,5},{13,9},{6,2},{10,6},{14,10},{7,3},{... | collective-permute-start | bytes 39944 | tf_op jit(solution)/shard_map/ppermute | solution.py:19
  141.0 40.9 %copy-start.41 = (f32[48,256]{1,0:T(8,128)S(1)}, f32[48,256]{1,0:T(8,128)}, u32[]{:S(2)}) copy-start(f32[48,256]{1,0:T(8,128)} %param.11) | copy-start | bytes 147460
  141.1 40.9 %copy-start.45 = (f32[48]{0:T(128)S(1)}, f32[48]{0:T(128)}, u32[]{:S(2)}) copy-start(f32[48]{0:T(128)} %param.13) | copy-start | bytes 580
  185.8 2.6 collective-permute-start.16
  187.1 3.1 collective-permute-start.17
  190.5 12.7 %collective-permute-start.18 = (f32[16,52,2]{2,0,1:T(8,128)S(1)}, f32[16,52,2]{2,0,1:T(8,128)S(1)}, u32[]{:S(2)}, u32[]{:S(2)}) collective-permute-start(f32[16,52,2]{2,0,1:T(8,128)S(1)} %get-tuple-element.94), channel_id=1, source_target_pairs={{0,4},{4,8},{8,12},{1,5},{5,9},{9,13},{2,6},{6,10},{10,14},{3,7},{... | collective-permute-start | bytes 19976 | tf_op jit(solution)/shard_map/ppermute | solution.py:17
  193.9 20.4 %collective-permute-start.19 = (f32[16,52,2]{2,0,1:T(8,128)S(1)}, f32[16,52,2]{2,0,1:T(8,128)S(1)}, u32[]{:S(2)}, u32[]{:S(2)}) collective-permute-start(f32[16,52,2]{2,0,1:T(8,128)S(1)} %get-tuple-element.93), channel_id=1, source_target_pairs={{4,0},{8,4},{12,8},{5,1},{9,5},{13,9},{6,2},{10,6},{14,10},{7,3},{... | collective-permute-start | bytes 19976 | tf_op jit(solution)/shard_map/ppermute | solution.py:19
  261.6 32.8 %copy-start.10 = (f32[16,48,256]{2,0,1:T(8,128)}, f32[16,48,256]{2,0,1:T(8,128)S(1)}, u32[]{:S(2)}) copy-start(f32[16,48,256]{2,0,1:T(8,128)S(1)} %multiply_add_fusion) | copy-start | bytes 2359300
  261.6 2.6 collective-permute-start.20
  262.9 3.1 collective-permute-start.21
  266.2 11.8 %collective-permute-start.22 = (f32[16,52,2]{2,0,1:T(8,128)S(1)}, f32[16,52,2]{2,0,1:T(8,128)S(1)}, u32[]{:S(2)}, u32[]{:S(2)}) collective-permute-start(f32[16,52,2]{2,0,1:T(8,128)S(1)} %get-tuple-element.92), channel_id=1, source_target_pairs={{0,4},{4,8},{8,12},{1,5},{5,9},{9,13},{2,6},{6,10},{10,14},{3,7},{... | collective-permute-start | bytes 19976 | tf_op jit(solution)/shard_map/ppermute | solution.py:17
  268.7 22.1 %collective-permute-start.23 = (f32[16,52,2]{2,0,1:T(8,128)S(1)}, f32[16,52,2]{2,0,1:T(8,128)S(1)}, u32[]{:S(2)}, u32[]{:S(2)}) collective-permute-start(f32[16,52,2]{2,0,1:T(8,128)S(1)} %get-tuple-element.91), channel_id=1, source_target_pairs={{4,0},{8,4},{12,8},{5,1},{9,5},{13,9},{6,2},{10,6},{14,10},{7,3},{... | collective-permute-start | bytes 19976 | tf_op jit(solution)/shard_map/ppermute | solution.py:19
  (40 other events, 452.7 us)
Sparse Core Ops, SparseCore 0:
  145.5 36.3 all-reduce.3
where the time goes:
time: 340 us; the launch traced here: 339 us
  waiting for transfers between devices  102 us (30%)
  blocking collectives  94.5 us (28%)
  starting transfers between devices  56.7 us (17%)
  other arithmetic  53.5 us (16%)
  between operations  15.7 us (5%)
  local copies, waits for them, and re-layouts  14.9 us (4%)
    ppermute x12, waiting for transfers between devices, padded_2(): lax.ppermute(head, axis, [((i + 1) % count, i) for i in range(ends)])  47.9 us
    ppermute x12, starting transfers between devices, padded_2(): lax.ppermute(tail, axis, [(i, (i + 1) % count) for i in range(ends)])  40.8 us
    psum x3, blocking collectives, solve_blocked(): lax.psum(jnp.stack([local_dot(residual, residual), local_dot(residual, ap...  40.2 us
    psum x1, waiting for transfers between devices, per_device(): material_next = (fixed_terms + lax.psum(absorbed_local, 'group')) / capacity  36.5 us
    psum x2, blocking collectives, per_device(): material_next = (fixed_terms + lax.psum(absorbed_local, 'group')) / capacity  34.5 us
    unnamed x1, blocking collectives  19.8 us
    ppermute x12, waiting for transfers between devices, padded_2(): lax.ppermute(tail, axis, [(i, (i + 1) % count) for i in range(ends)])  17.4 us
    ppermute x12, starting transfers between devices, padded_2(): lax.ppermute(head, axis, [((i + 1) % count, i) for i in range(ends)])  15.9 us
  transfers between devices with their start and end apart: 25, of which 12 were waited for; matrix products, arithmetic and copies ran while one was open for 3% of the time, Pallas kernels for 0%

commit v1 on v0

v1 whole, which is shorter than its diff:
```python
import functools

import jax
import jax.numpy as jnp
from jax import lax
from jax.experimental import pallas as pl
from jax.experimental.pallas import tpu as pltpu
from jax.sharding import PartitionSpec as P

ITERS = 3
LANES = 128
SUB = 8
MESH = pl.DeviceIdType.MESH
HI = lax.Precision.HIGHEST


def harm(a, b):
    total = a + b
    return 2.0 * a * b / jnp.where(total > 0.0, total, 1.0)


def kernel(
    nr, npol, nz,
    dens, opac, rad, mat0, wts, flux,
    e_out, m_out, col_out,
    e_x, a_x, d_x, r_x, dg_x, fu_x, fd_x, fl_x, fr_x, ar, aar,
    o_ea, hl_ea, hr_ea, o_d, hl_d, hr_d, o_r, hl_r, hr_r,
    halo_x, halo_ar, gsum, gram, cres, cimg,
    rows_src, rows_buf, absb, emis, rsbuf, mnext, fixed, capac, dmat,
    slab_s, slab_v, pol_s, pol_v, diag_s, diag_v,
    gram_s, gram_v, rs_s, rs_v, ag_s, ag_v, row_s, row_v,
):
    ng, nrow, ncol = rad.shape
    nt = ncol // LANES
    next_ = nrow + 2 * SUB
    own = slice(SUB, SUB + nrow)
    tiles = (nrow // SUB) * nt
    tp = tiles // nz
    plane = nr * npol

    ir = lax.axis_index("radius")
    ip = lax.axis_index("polar")
    iz = lax.axis_index("group")
    me = ir * npol + ip

    def lane_of(n):
        return lax.broadcasted_iota(jnp.int32, (n, LANES), 1)

    lane_own, lane_ext = lane_of(nrow), lane_of(next_)

    def zeros_at(ref, *idx):
        ref[idx] = jnp.zeros(ref.at[idx].shape, ref.dtype)

    for ref in (e_x, a_x, d_x, r_x):
        zeros_at(ref, slice(None), slice(0, SUB), slice(None))
        zeros_at(ref, slice(None), slice(SUB + nrow, next_), slice(None))
    for ref in (hl_ea, hr_ea, hl_d, hr_d, hl_r, hr_r, rows_buf):
        ref[...] = jnp.zeros(ref.shape, ref.dtype)

    barrier = pltpu.get_barrier_semaphore()

    def plane_id(k):
        other = lax.rem(me + k, plane)
        return other, {"radius": other // npol, "polar": lax.rem(other, npol)}

    @pl.loop(1, plane)
    def _(k):
        _, where = plane_id(k)
        pl.semaphore_signal(barrier, inc=1, device_id=where, device_id_type=MESH)

    for k in range(1, nz):
        pl.semaphore_signal(
            barrier, inc=1, device_id={"group": lax.rem(iz + k, nz)}, device_id_type=MESH
        )

    def remote(src, dst, ssem, rsem, where):
        return pltpu.make_async_remote_copy(
            src_ref=src, dst_ref=dst, send_sem=ssem, recv_sem=rsem,
            device_id=where, device_id_type=MESH,
        )

    def near(dr, dp):
        return {"radius": lax.rem(ir + dr + nr, nr), "polar": lax.rem(ip + dp + npol, npol)}

    def inside(dr, dp):
        r, p = ir + dr, ip + dp
        return (r >= 0) & (r < nr) & (p >= 0) & (p < npol)

    def slab_copies(src_ref, lo, hi, dst_ref, f):
        out = []
        for i, dr in enumerate((-1, 1)):
            src = src_ref.at[:, pl.ds(lo if dr < 0 else hi, SUB), :]
            dst = dst_ref.at[:, pl.ds(SUB + nrow if dr < 0 else 0, SUB), :]
            out.append((dr, 0, remote(src, dst, slab_s.at[f, i], slab_v.at[f, i], near(dr, 0))))
        return out

    def pol_copies(o, hl, hr, f):
        out = []
        for i, dp in enumerate((-1, 1)):
            dst = (hr if dp < 0 else hl).at[:, pl.ds(SUB, nrow), :]
            out.append((0, dp, remote(o, dst, pol_s.at[f, i], pol_v.at[f, i], near(0, dp))))
        return out

    def diag_copies(o, hl, hr, f):
        out = []
        for i, (dr, dp) in enumerate(((-1, -1), (-1, 1), (1, -1), (1, 1))):
            src = o.at[:, pl.ds(0 if dr < 0 else nrow - SUB, SUB), :]
            dst = (hr if dp < 0 else hl).at[:, pl.ds(SUB + nrow if dr < 0 else 0, SUB), :]
            out.append((dr, dp, remote(src, dst, diag_s.at[f, i], diag_v.at[f, i], near(dr, dp))))
        return out

    def start(copies):
        for dr, dp, c in copies:
            @pl.when(inside(dr, dp))
            def _():
                c.start()

    def finish(copies):
        for dr, dp, c in copies:
            @pl.when(inside(-dr, -dp))
            def _():
                c.wait_recv()
        for dr, dp, c in copies:
            @pl.when(inside(dr, dp))
            def _():
                c.wait_send()

    def load(ref, g, rows):
        return [ref[g, rows, k * LANES:(k + 1) * LANES] for k in range(nt)]

    def pack(tiles_in, g, into):
        left = pltpu.roll(tiles_in[0], 2 * g, 1)
        right = pltpu.roll(tiles_in[-1], lax.rem(2 * g + LANES // 2 + 2, LANES), 1)
        half = lane_own // 2
        into = jnp.where(half == g, left, into)
        return jnp.where(half == g + LANES // 4, right, into)

    def left_of(v, halo, g):
        n = v[0].shape[0]
        edge = lane_of(n) == 0
        turned = [pltpu.roll(t, 1, 1) for t in v]
        before = [pltpu.roll(halo, LANES // 2 - 1 - 2 * g, 1)] + turned[:-1]
        return [jnp.where(edge, b, t) for b, t in zip(before, turned)]

    def right_of(v, halo, g):
        n = v[0].shape[0]
        edge = lane_of(n) == LANES - 1
        turned = [pltpu.roll(t, LANES - 1, 1) for t in v]
        after = turned[1:] + [pltpu.roll(halo, LANES - 1 - 2 * g, 1)]
        return [jnp.where(edge, b, t) for b, t in zip(after, turned)]

    def above(t):
        return pltpu.roll(t, 1, 0)

    def below(t):
        return pltpu.roll(t, t.shape[0] - 1, 0)

    def both(hl, hr, k):
        return jnp.where(lane_ext < LANES // 2, hr[k], hl[k])

    def outer_of(x):
        n = x.shape[0]
        return jnp.where(lane_of(n) < LANES // 2, pltpu.roll(x, LANES - 1, 1), pltpu.roll(x, 1, 1))

    def inner_of(o):
        return jnp.where(
            lane_own < LANES // 2,
            pltpu.roll(o, LANES // 2 - 1, 1),
            pltpu.roll(o, LANES // 2 + 1, 1),
        )

    zero_pack = jnp.zeros((nrow, LANES), jnp.float32)
    zero_tiles = tuple(jnp.zeros((nrow, LANES), jnp.float32) for _ in range(nt))

    def put_tiles(ref, parts):
        for k, part in enumerate(parts):
            for i in range(nrow // SUB):
                ref[k * (nrow // SUB) + i] = part[i * SUB:(i + 1) * SUB]

    def get_tiles(ref):
        per = nrow // SUB
        return [
            jnp.concatenate([ref[k * per + i] for i in range(per)], axis=0) for k in range(nt)
        ]

    def scatter_copies(src, slot):
        out = []
        for k in range(1, nz):
            to = lax.rem(iz + k, nz)
            out.append(remote(
                src.at[pl.ds(to * tp, tp)], rsbuf.at[slot, iz],
                rs_s.at[slot, k], rs_v.at[slot, k], {"group": to},
            ))
        return out

    def gathered_sum(src, slot, copies):
        rsbuf[slot, iz] = src[pl.ds(iz * tp, tp)]
        for c in copies:
            c.wait_recv()
        total = rsbuf[slot, 0]
        for k in range(1, nz):
            total = total + rsbuf[slot, k]
        return total

    dens_t = [dens[:, k * LANES:(k + 1) * LANES] for k in range(nt)]

    def first(g, carry):
        oe, oa, em = carry
        a = [
            opac[g, :, k * LANES:(k + 1) * LANES].astype(jnp.float32) * dens_t[k]
            for k in range(nt)
        ]
        for k in range(nt):
            a_x[g, own, k * LANES:(k + 1) * LANES] = a[k]
            e_x[g, own, k * LANES:(k + 1) * LANES] = rad[g, :, k * LANES:(k + 1) * LANES]
        em = tuple(em[k] + a[k] * wts[g] for k in range(nt))
        return pack(load(rad, g, slice(None)), g, oe), pack(a, g, oa), em

    oe, oa, em = lax.fori_loop(0, ng, first, (zero_pack, zero_pack, zero_tiles))
    o_ea[0] = oe
    o_ea[1] = oa
    put_tiles(emis, em)
    rows = sum(jnp.sum(t, axis=1, keepdims=True) for t in dens_t)
    rows_src[...] = jnp.broadcast_to(rows, (nrow, LANES))

    pl.semaphore_wait(barrier, plane - 1 + nz - 1)

    ea = (
        slab_copies(e_x, SUB, nrow, e_x, 0)
        + slab_copies(a_x, SUB, nrow, a_x, 1)
        + pol_copies(o_ea, hl_ea, hr_ea, 0)
    )
    start(ea)
    emit = scatter_copies(emis, ITERS)
    for c in emit:
        c.start()
    prefix = []
    for k in range(1, npol):
        to = lax.rem(ip + k, npol)
        prefix.append((
            ip + k < npol, ip - k >= 0,
            remote(rows_src, rows_buf.at[ip], row_s.at[k], row_v.at[k], {"polar": to}),
        ))
    for sends, _, c in prefix:
        @pl.when(sends)
        def _():
            c.start()

    tri = (
        lax.broadcasted_iota(jnp.int32, (ncol, ncol), 0)
        <= lax.broadcasted_iota(jnp.int32, (ncol, ncol), 1)
    ).astype(jnp.float32)
    within = jnp.dot(dens[...], tri, precision=HI, preferred_element_type=jnp.float32)
    col_out[...] = within
    finish(ea)

    x_e = both(hl_ea, hr_ea, 0)
    x_a = both(hl_ea, hr_ea, 1)
    halo_x[...] = x_e

    def second(g, od):
        v = load(e_x, g, slice(None))
        a = load(a_x, g, own)
        x = halo_x[own]
        v_own = [t[own] for t in v]
        lft, rgt = left_of(v_own, x, g), right_of(v_own, x, g)
        d = []
        for k in range(nt):
            rs = 0.5 * (below(v[k])[own] - above(v[k])[own])
            ps = 0.5 * (rgt[k] - lft[k])
            s = jnp.sqrt(rs * rs + ps * ps)
            q = a[k] * v_own[k]
            d.append(v_own[k] * (2.0 * q + s) / (6.0 * q * q + 3.0 * q * s + s * s))
            d_x[g, own, k * LANES:(k + 1) * LANES] = d[k]
        return pack(d, g, od)

    o_d[0] = lax.fori_loop(0, ng, second, zero_pack)
    dd = slab_copies(d_x, SUB, nrow, d_x, 2) + pol_copies(o_d, hl_d, hr_d, 1) + diag_copies(
        o_d, hl_d, hr_d, 0
    )
    start(dd)

    for _, comes, c in prefix:
        @pl.when(comes)
        def _():
            c.wait_recv()
    carried = rows_buf[0]
    for k in range(1, npol):
        carried = carried + rows_buf[k]
    diag = (
        lax.broadcasted_iota(jnp.int32, (nrow, nrow), 0)
        == lax.broadcasted_iota(jnp.int32, (nrow, nrow), 1)
    )
    flux_col = jnp.sum(jnp.where(diag, flux[...], 0.0), axis=1, keepdims=True)
    fix = []
    for k in range(nt):
        sl = slice(k * LANES, (k + 1) * LANES)
        column = (2.0 / (ncol * npol)) * (carried + col_out[:, sl])
        col_out[:, sl] = column
        fix.append(
            16.0 * dens_t[k] * mat0[:, sl] + flux_col * dens_t[k] * jnp.exp(-column)
        )
    put_tiles(fixed, fix)
    put_tiles(capac, [16.0 * t for t in dens_t])
    emission = gathered_sum(emis, ITERS, emit)
    mine = pl.ds(iz * tp, tp)
    capac[mine] = capac[mine] + emission
    finish(dd)

    x_d = both(hl_d, hr_d, 0)
    d_in, d_out = inner_of(o_d[0]), outer_of(x_d)[own]
    x_mid = x_d[own]
    p_in, p_out = harm(x_mid, d_in), harm(x_mid, d_out)
    p_up, p_dn = harm(x_mid, above(x_d)[own]), harm(x_mid, below(x_d)[own])
    p_dg = 1.0 + x_a[own] + p_in + p_out + p_up + p_dn
    halo_ar[0] = p_in
    halo_ar[1] = p_out
    halo_ar[2] = p_up
    halo_ar[3] = p_dn
    halo_ar[4] = p_dg
    gsum[...] = jnp.zeros(gsum.shape, jnp.float32)
    mat_t = [mat0[:, k * LANES:(k + 1) * LANES] for k in range(nt)]
    d_halo = aar
    del d_halo
    hl_d[0] = x_d

    def third(g, o):
        d = load(d_x, g, slice(None))
        a = load(a_x, g, slice(None))
        v = load(e_x, g, slice(None))
        x = hl_d[0]
        xe = halo_x[own]
        dl, dr = left_of(d, x, g), right_of(d, x, g)
        v_own = [t[own] for t in v]
        vl, vr = left_of(v_own, xe, g), right_of(v_own, xe, g)
        res = []
        for k in range(nt):
            sl = slice(k * LANES, (k + 1) * LANES)
            fl, fr, fu = harm(d[k], dl[k]), harm(d[k], dr[k]), harm(d[k], above(d[k]))
            fd = below(fu)
            dg = 1.0 + a[k] + fl + fr + fu + fd
            fl_x[g, :, sl] = fl
            fr_x[g, :, sl] = fr
            fu_x[g, :, sl] = fu
            fd_x[g, :, sl] = fd
            dg_x[g, :, sl] = dg
            c = v_own[k]
            ao = a[k][own]
            image = (
                (1.0 + ao) * c
                + fu[own] * (c - above(v[k])[own])
                + fd[own] * (c - below(v[k])[own])
                + fl[own] * (c - vl[k])
                + fr[own] * (c - vr[k])
            )
            r = ao * wts[g] * mat_t[k] + c - image
            res.append(r)
            r_x[g, own, sl] = r
            e_out[g, :, sl] = c
        return pack(res, g, o)

    o_r[0] = lax.fori_loop(0, ng, third, zero_pack)
    m_out[...] = mat0[...]

    ones = jnp.ones((SUB, LANES), jnp.float32)
    quants = 4 * ng
    pick = (
        lax.broadcasted_iota(jnp.int32, (quants, LANES), 0)
        == lax.broadcasted_iota(jnp.int32, (quants, LANES), 1)
    )

    @pl.loop(0, ITERS)
    def _(it):
        rr = slab_copies(r_x, SUB, nrow, r_x, 3) + pol_copies(o_r, hl_r, hr_r, 2) + diag_copies(
            o_r, hl_r, hr_r, 1
        )
        start(rr)
        finish(rr)
        x_r = both(hl_r, hr_r, 0)
        halo_x[...] = x_r
        x_own = x_r[own]
        halo_ar[5] = (
            halo_ar[4] * x_own
            - halo_ar[0] * inner_of(o_r[0])
            - halo_ar[1] * outer_of(x_r)[own]
            - halo_ar[2] * above(x_r)[own]
            - halo_ar[3] * below(x_r)[own]
        )

        @pl.loop(0, ng)
        def _(g):
            v = load(r_x, g, slice(None))
            x = halo_x[...]
            vl, vr = left_of(v, x, g), right_of(v, x, g)
            w = []
            for k in range(nt):
                sl = slice(k * LANES, (k + 1) * LANES)
                w.append(
                    dg_x[g, :, sl] * v[k]
                    - fu_x[g, :, sl] * above(v[k])
                    - fd_x[g, :, sl] * below(v[k])
                    - fl_x[g, :, sl] * vl[k]
                    - fr_x[g, :, sl] * vr[k]
                )
            w_own = [t[own] for t in w]
            wx = halo_ar[5]
            wl, wr = left_of(w_own, wx, g), right_of(w_own, wx, g)
            sums = [0.0, 0.0, 0.0, 0.0]
            for k in range(nt):
                sl = slice(k * LANES, (k + 1) * LANES)
                c = w_own[k]
                t = (
                    dg_x[g, own, sl] * c
                    - fu_x[g, own, sl] * above(w[k])[own]
                    - fd_x[g, own, sl] * below(w[k])[own]
                    - fl_x[g, own, sl] * wl[k]
                    - fr_x[g, own, sl] * wr[k]
                )
                ar[g, :, sl] = c
                aar[g, :, sl] = t
                r = v[k][own]
                for i, (p, q) in enumerate(((r, r), (r, c), (c, c), (c, t))):
                    sums[i] = sums[i] + jnp.sum(p * q, axis=0, keepdims=True)
            for i in range(4):
                gsum[pl.ds(i * ng + g, 1), :] = sums[i]

        gram[it, me] = lax.dot_general(
            ones, gsum[...], (((1,), (1,)), ((), ())), precision=HI,
            preferred_element_type=jnp.float32,
        )

        def gram_copy(k):
            _, where = plane_id(k)
            return remote(
                gram.at[it, me], gram.at[it, me], gram_s.at[k], gram_v.at[it, k], where
            )

        @pl.loop(1, plane)
        def _(k):
            gram_copy(k).start()

        @pl.loop(1, plane)
        def _(k):
            c = gram_copy(k)
            c.wait_recv()
            c.wait_send()

        total = lax.fori_loop(
            0, plane, lambda k, s: s + gram[it, k], jnp.zeros((SUB, LANES), jnp.float32)
        )
        spread = jnp.sum(jnp.where(pick, total[0:1], 0.0), axis=1, keepdims=True)
        norm_first = spread[0:ng]
        first_curv = spread[ng:2 * ng]
        image_norm = spread[2 * ng:3 * ng]
        image_twice = spread[3 * ng:4 * ng]
        step_first = norm_first / first_curv
        norm_second = (
            norm_first - 2.0 * step_first * first_curv + step_first * step_first * image_norm
        )
        scaled = 1.0 + norm_second / norm_first
        second_curv = (
            scaled * scaled * first_curv
            - scaled * step_first * (2.0 * image_norm)
            + step_first * step_first * image_twice
        )
        step_second = norm_second / second_curv
        cres[...] = jnp.broadcast_to(step_first + step_second * scaled, (ng, LANES))
        cimg[...] = jnp.broadcast_to(step_second * step_first, (ng, LANES))

        def update(g, absorbed):
            cr = cres[pl.ds(g, 1), :]
            ci = cimg[pl.ds(g, 1), :]
            out = []
            for k in range(nt):
                sl = slice(k * LANES, (k + 1) * LANES)
                r, w = r_x[g, own, sl], ar[g, :, sl]
                e = e_out[g, :, sl] + cr * r - ci * w
                e_out[g, :, sl] = e
                r_x[g, own, sl] = r - cr * w + ci * aar[g, :, sl]
                out.append(absorbed[k] + a_x[g, own, sl] * e)
            return tuple(out)

        put_tiles(absb, lax.fori_loop(0, ng, update, zero_tiles))
        send = scatter_copies(absb, it)
        for c in send:
            c.start()
        mnext[it, mine] = (fixed[mine] + gathered_sum(absb, it, send)) / capac[mine]
        give = []
        for k in range(1, nz):
            give.append(remote(
                mnext.at[it, mine], mnext.at[it, mine],
                ag_s.at[it, k], ag_v.at[it, k], {"group": lax.rem(iz + k, nz)},
            ))
        for c in give:
            c.start()
        for c in give:
            c.wait_recv()
        for c in give + send:
            c.wait_send()
        news = get_tiles(mnext.at[it])
        for k in range(nt):
            sl = slice(k * LANES, (k + 1) * LANES)
            dmat[:, sl] = news[k] - m_out[:, sl]
            m_out[:, sl] = news[k]

        @pl.when(it + 1 < ITERS)
        def _():
            def feed(g, o):
                res = []
                for k in range(nt):
                    sl = slice(k * LANES, (k + 1) * LANES)
                    r = r_x[g, own, sl] + a_x[g, own, sl] * wts[g] * dmat[:, sl]
                    r_x[g, own, sl] = r
                    res.append(r)
                return pack(res, g, o)

            o_r[0] = lax.fori_loop(0, ng, feed, zero_pack)

    for c in emit:
        c.wait_send()
    for sends, _, c in prefix:
        @pl.when(sends)
        def _():
            c.wait_send()


def per_device(nr, npol, nz, density, opacity, radiation_old, material_old, weights, stellar_flux):
    ng, nrow, ncol = radiation_old.shape
    f32 = jnp.float32
    ext, inner = (ng, nrow + 2 * SUB, ncol), (ng, nrow, ncol)
    tiles = (nrow // SUB) * (ncol // LANES)
    plane = nr * npol
    vm = lambda *shape: pltpu.VMEM(shape, f32)
    packed, around = (nrow, LANES), (nrow + 2 * SUB, LANES)
    dma = lambda *shape: pltpu.SemaphoreType.DMA(shape)
    scratch = (
        [vm(*ext) for _ in range(9)]
        + [vm(*inner), vm(*inner)]
        + [vm(2, *packed), vm(2, *around), vm(2, *around)]
        + [vm(1, *packed), vm(1, *around), vm(1, *around)] * 2
        + [vm(*around), vm(6, *packed), vm(LANES, LANES), vm(ITERS, plane, SUB, LANES)]
        + [vm(ng, LANES), vm(ng, LANES)]
        + [vm(*packed), vm(npol, *packed), vm(tiles, SUB, LANES), vm(tiles, SUB, LANES)]
        + [vm(ITERS + 1, nz, tiles // nz, SUB, LANES), vm(ITERS, tiles, SUB, LANES)]
        + [vm(tiles, SUB, LANES), vm(tiles, SUB, LANES), vm(nrow, ncol)]
        + [dma(4, 2), dma(4, 2), dma(3, 2), dma(3, 2), dma(2, 4), dma(2, 4)]
        + [dma(plane), dma(ITERS, plane), dma(ITERS + 1, nz), dma(ITERS + 1, nz)]
        + [dma(ITERS, nz), dma(ITERS, nz), dma(npol), dma(npol)]
    )
    in_vmem = pl.BlockSpec(memory_space=pltpu.VMEM)
    return pl.pallas_call(
        functools.partial(kernel, nr, npol, nz),
        out_shape=[
            jax.ShapeDtypeStruct(inner, f32),
            jax.ShapeDtypeStruct((nrow, ncol), f32),
            jax.ShapeDtypeStruct((nrow, ncol), f32),
        ],
        in_specs=[in_vmem] * 4 + [pl.BlockSpec(memory_space=pltpu.SMEM), in_vmem],
        out_specs=[in_vmem] * 3,
        scratch_shapes=scratch,
        compiler_params=pltpu.CompilerParams(
            collective_id=0, has_side_effects=True, vmem_limit_bytes=48 * 1024 * 1024
        ),
    )(density, opacity, radiation_old, material_old, weights, stellar_flux.reshape(1, -1))


def solution(mesh):
    sizes = (mesh.shape["radius"], mesh.shape["polar"], mesh.shape["group"])
    return jax.shard_map(
        functools.partial(per_device, *sizes),
        mesh=mesh,
        in_specs=(
            P("radius", "polar"),
            P("group", "radius", "polar"),
            P("group", "radius", "polar"),
            P("radius", "polar"),
            P("group"),
            P("radius"),
        ),
        out_specs=(P("group", "radius", "polar"), P("radius", "polar"), P("radius", "polar")),
        check_vma=False,
    )
```

time: 340 us -> 86.5 us (0.25)
  waiting for transfers between devices: 102 us -> 0 us
  blocking collectives: 94.5 us -> 0 us
  Pallas kernels: 0 us -> 79 us
  starting transfers between devices: 56.7 us -> 0 us
  other arithmetic: 53.5 us -> 0 us
  between operations: 15.7 us -> 0.66 us
  local copies, waits for them, and re-layouts: 14.9 us -> 6.5 us
    pallas_call x0 -> x1, Pallas kernels: none -> 79 us  [per_device(): pl.pallas_call(functools.partial(kernel, nr, npol, nz), out_shape=[jax.Sh...]
    psum x5 -> x0, blocking collectives: 74.7 us -> none  [the longest x3 40.2 us: solve_blocked(): lax.psum(jnp.stack([local_dot(residual, residual), local_dot(residual, ap...]
    ppermute x24 -> x0, waiting for transfers between devices: 65.3 us -> none  [the longest x12 47.9 us: padded_2(): lax.ppermute(head, axis, [((i + 1) % count, i) for i in range(ends)])]
    ppermute x24 -> x0, starting transfers between devices: 56.7 us -> none  [the longest x12 40.8 us: padded_2(): lax.ppermute(tail, axis, [(i, (i + 1) % count) for i in range(ends)])]
    psum x1 -> x0, waiting for transfers between devices: 36.5 us -> none  [per_device(): material_next = (fixed_terms + lax.psum(absorbed_local, 'group')) / capacity]
    reduce_sum x7 -> x0, other arithmetic: 23 us -> none  [the longest x3 13.4 us: local_dot(): return jnp.sum(left_field * right_field, axis=(1, 2))]
    unnamed x1 -> x0, blocking collectives: 19.8 us -> none
    add x11 -> x0, other arithmetic: 16.3 us -> none  [the longest x3 11.8 us: apply_padded(): (1.0 + absorb) * field + face_coeffs[0] * (field - padded[:, 2:, 1:-1])]
  transfers between devices with their start and end apart: 25 -> 0, of which waited for: 12 -> 0; matrix products, arithmetic and copies ran while one was open for 3% -> 0% of each run, Pallas kernels for 0% -> 0%
where the time goes in v1:
time: 86.5 us; the launch traced here: 86.2 us
  Pallas kernels  79 us (91%)
  local copies, waits for them, and re-layouts  6.5 us (8%)
    pallas_call x1, Pallas kernels, per_device(): pl.pallas_call(functools.partial(kernel, nr, npol, nz), out_shape=[jax.Sh...  79 us
    unnamed x15, local copies, waits for them, and re-layouts  6.5 us

profile of v1, /device:TPU:0, one launch (start us, length us, event | category | flops | bytes accessed | tf_op | source)
XLA Modules:
  0.0 86.2 jit_solution(4480500495116051189)
XLA Ops:
  0.6 0.0 copy-start.5
  0.6 0.0 copy-start.4
  0.7 0.6 copy-done.5
  1.3 0.0 copy-done.4
  1.3 0.0 copy-start
  1.3 1.1 %copy-done = f32[16,48,256]{2,1,0:T(8,128)S(1)} copy-done((f32[16,48,256]{2,1,0:T(8,128)S(1)}, f32[16,48,256]{2,1,0:T(8,128)}, u32[]{:S(2)}) %copy-start) | copy-done | bytes 786456
  2.4 0.0 copy-start.1
  2.4 1.0 %copy-done.1 = bf16[16,48,256]{2,1,0:T(8,128)(2,1)S(1)} copy-done((bf16[16,48,256]{2,1,0:T(8,128)(2,1)S(1)}, bf16[16,48,256]{2,1,0:T(8,128)(2,1)}, u32[]{:S(2)}) %copy-start.1) | copy-done | bytes 393240
  3.4 0.0 copy-start.2
  3.4 0.8 copy-done.2
  4.2 0.0 copy-start.3
  4.2 0.8 copy-done.3
  5.0 79.0 %shard_map.85 = (f32[16,48,256]{2,1,0:T(8,128)S(1)}, f32[48,256]{1,0:T(8,128)S(1)}, f32[48,256]{1,0:T(8,128)S(1)}) custom-call(f32[48,256]{1,0:T(8,128)S(1)} %copy-done.2, bf16[16,48,256]{2,1,0:T(8,128)(2,1)S(1)} %copy-done.1, f32[16,48,256]{2,1,0:T(8,128)S(1)} %copy-done, f32[48,256]{1,0:T(8,128)S(1)} %copy-done.3, f32[16]{0:T(128)S(1)} %copy-done.4, ...), custom_call_target="tpu_custom_call" | custom-call | tf_op jit(solution)/shard_map/pallas_call | solution.py:551
  84.1 0.9 %copy.12 = f32[16,48,256]{2,1,0:T(8,128)} copy(f32[16,48,256]{2,1,0:T(8,128)S(1)} %get-tuple-element.6) | data formatting | bytes 1572864
  84.9 0.6 copy.13
  85.6 0.6 copy.14
Async XLA Ops:
  0.6 0.7 copy-start.5
  0.6 0.7 copy-start.4
  1.3 1.1 %copy-start = (f32[16,48,256]{2,1,0:T(8,128)S(1)}, f32[16,48,256]{2,1,0:T(8,128)}, u32[]{:S(2)}) copy-start(f32[16,48,256]{2,1,0:T(8,128)} %rad.1) | copy-start | bytes 2359300
  2.4 1.0 %copy-start.1 = (bf16[16,48,256]{2,1,0:T(8,128)(2,1)S(1)}, bf16[16,48,256]{2,1,0:T(8,128)(2,1)}, u32[]{:S(2)}) copy-start(bf16[16,48,256]{2,1,0:T(8,128)(2,1)} %opac.1) | copy-start | bytes 1179652
  3.4 0.8 copy-start.2
  4.2 0.8 copy-start.3

commit v2 on v1

--- a/solution.py
+++ b/solution.py
@@ -25,7 +25,7 @@
     e_out, m_out, col_out,
     e_x, a_x, d_x, r_x, dg_x, fu_x, fd_x, fl_x, fr_x, ar, aar,
     o_ea, hl_ea, hr_ea, o_d, hl_d, hr_d, o_r, hl_r, hr_r,
-    halo_x, halo_ar, gsum, gram, cres, cimg,
+    o_aw, halo_x, halo_ar, gsum, gram, cres, cimg,
     rows_src, rows_buf, absb, emis, rsbuf, mnext, fixed, capac, dmat,
     slab_s, slab_v, pol_s, pol_v, diag_s, diag_v,
     gram_s, gram_v, rs_s, rs_v, ag_s, ag_v, row_s, row_v,
@@ -188,13 +188,13 @@
         for k in range(1, nz):
             to = lax.rem(iz + k, nz)
             out.append(remote(
-                src.at[pl.ds(to * tp, tp)], rsbuf.at[slot, iz],
+                src, rsbuf.at[slot, iz],
                 rs_s.at[slot, k], rs_v.at[slot, k], {"group": to},
             ))
         return out
 
     def gathered_sum(src, slot, copies):
-        rsbuf[slot, iz] = src[pl.ds(iz * tp, tp)]
+        rsbuf[slot, iz] = src[...]
         for c in copies:
             c.wait_recv()
         total = rsbuf[slot, 0]
@@ -205,7 +205,7 @@
     dens_t = [dens[:, k * LANES:(k + 1) * LANES] for k in range(nt)]
 
     def first(g, carry):
-        oe, oa, em = carry
+        oe, oa, ow, em = carry
         a = [
             opac[g, :, k * LANES:(k + 1) * LANES].astype(jnp.float32) * dens_t[k]
             for k in range(nt)
@@ -213,10 +213,12 @@
         for k in range(nt):
             a_x[g, own, k * LANES:(k + 1) * LANES] = a[k]
             e_x[g, own, k * LANES:(k + 1) * LANES] = rad[g, :, k * LANES:(k + 1) * LANES]
-        em = tuple(em[k] + a[k] * wts[g] for k in range(nt))
-        return pack(load(rad, g, slice(None)), g, oe), pack(a, g, oa), em
-
-    oe, oa, em = lax.fori_loop(0, ng, first, (zero_pack, zero_pack, zero_tiles))
+        aw = [t * wts[g] for t in a]
+        em = tuple(em[k] + aw[k] for k in range(nt))
+        return pack(load(rad, g, slice(None)), g, oe), pack(a, g, oa), pack(aw, g, ow), em
+
+    oe, oa, ow, em = lax.fori_loop(0, ng, first, (zero_pack, zero_pack, zero_pack, zero_tiles))
+    o_aw[...] = ow
     o_ea[0] = oe
     o_ea[1] = oa
     put_tiles(emis, em)
@@ -303,7 +305,7 @@
     put_tiles(fixed, fix)
     put_tiles(capac, [16.0 * t for t in dens_t])
     emission = gathered_sum(emis, ITERS, emit)
-    mine = pl.ds(iz * tp, tp)
+    mine = pl.ds(0, tiles)
     capac[mine] = capac[mine] + emission
     finish(dd)
 
@@ -319,9 +321,6 @@
     halo_ar[3] = p_dn
     halo_ar[4] = p_dg
     gsum[...] = jnp.zeros(gsum.shape, jnp.float32)
-    mat_t = [mat0[:, k * LANES:(k + 1) * LANES] for k in range(nt)]
-    d_halo = aar
-    del d_halo
     hl_d[0] = x_d
 
     def third(g, o):
@@ -353,7 +352,7 @@
                 + fl[own] * (c - vl[k])
                 + fr[own] * (c - vr[k])
             )
-            r = ao * wts[g] * mat_t[k] + c - image
+            r = c - image
             res.append(r)
             r_x[g, own, sl] = r
             e_out[g, :, sl] = c
@@ -361,6 +360,7 @@
 
     o_r[0] = lax.fori_loop(0, ng, third, zero_pack)
     m_out[...] = mat0[...]
+    dmat[...] = mat0[...]
 
     ones = jnp.ones((SUB, LANES), jnp.float32)
     quants = 4 * ng
@@ -371,11 +371,59 @@
 
     @pl.loop(0, ITERS)
     def _(it):
-        rr = slab_copies(r_x, SUB, nrow, r_x, 3) + pol_copies(o_r, hl_r, hr_r, 2) + diag_copies(
-            o_r, hl_r, hr_r, 1
-        )
-        start(rr)
-        finish(rr)
+        lo, hi = dmat[:, :LANES], dmat[:, ncol - LANES:]
+        even = lane_own % 2 == 0
+        first_two = jnp.where(even, lo[:, 0:1], lo[:, 1:2])
+        last_two = jnp.where(even, hi[:, LANES - 2:LANES - 1], hi[:, LANES - 1:LANES])
+        o_r[0] = o_r[0] + o_aw[...] * jnp.where(lane_own < LANES // 2, first_two, last_two)
+        sides = pol_copies(o_r, hl_r, hr_r, 2) + diag_copies(o_r, hl_r, hr_r, 1)
+        slabs = slab_copies(r_x, SUB, nrow, r_x, 3)
+        start(sides)
+
+        @pl.loop(0, ng)
+        def _(g):
+            for base in (0, nrow - SUB):
+                rows_x, rows_m = slice(SUB + base, 2 * SUB + base), slice(base, base + SUB)
+                r_x[g, rows_x, :] = r_x[g, rows_x, :] + a_x[g, rows_x, :] * wts[g] * dmat[rows_m, :]
+
+        start(slabs)
+        mid = slice(2 * SUB, nrow)
+        mid_m = slice(SUB, nrow - SUB)
+        no_halo = jnp.zeros((nrow - 2 * SUB, LANES), jnp.float32)
+
+        def stencil(g, rows, v, up, dn, vl, vr):
+            out = []
+            for k in range(nt):
+                sl = slice(k * LANES, (k + 1) * LANES)
+                out.append(
+                    dg_x[g, rows, sl] * v[k]
+                    - fu_x[g, rows, sl] * up[k]
+                    - fd_x[g, rows, sl] * dn[k]
+                    - fl_x[g, rows, sl] * vl[k]
+                    - fr_x[g, rows, sl] * vr[k]
+                )
+            return out
+
+        @pl.loop(0, ng)
+        def _(g):
+            v, full = [], []
+            for k in range(nt):
+                sl = slice(k * LANES, (k + 1) * LANES)
+                r = r_x[g, mid, sl] + a_x[g, mid, sl] * wts[g] * dmat[mid_m, sl]
+                r_x[g, mid, sl] = r
+                v.append(r)
+                full.append(jnp.concatenate(
+                    [r_x[g, SUB:2 * SUB, sl], r, r_x[g, nrow:nrow + SUB, sl]], axis=0
+                ))
+            inner = slice(SUB, nrow - SUB)
+            w = stencil(
+                g, mid, v, [above(t)[inner] for t in full], [below(t)[inner] for t in full],
+                left_of(v, no_halo, g), right_of(v, no_halo, g),
+            )
+            for k in range(nt):
+                ar[g, mid_m, k * LANES:(k + 1) * LANES] = w[k]
+
+        finish(sides + slabs)
         x_r = both(hl_r, hr_r, 0)
         halo_x[...] = x_r
         x_own = x_r[own]
@@ -389,19 +437,28 @@
 
         @pl.loop(0, ng)
         def _(g):
-            v = load(r_x, g, slice(None))
             x = halo_x[...]
-            vl, vr = left_of(v, x, g), right_of(v, x, g)
-            w = []
-            for k in range(nt):
-                sl = slice(k * LANES, (k + 1) * LANES)
-                w.append(
-                    dg_x[g, :, sl] * v[k]
-                    - fu_x[g, :, sl] * above(v[k])
-                    - fd_x[g, :, sl] * below(v[k])
-                    - fl_x[g, :, sl] * vl[k]
-                    - fr_x[g, :, sl] * vr[k]
+
+            def end_rows(rows, window, keep):
+                full = load(r_x, g, window)
+                v = [t[keep] for t in full]
+                return stencil(
+                    g, rows, v, [above(t)[keep] for t in full], [below(t)[keep] for t in full],
+                    left_of(v, x[rows], g), right_of(v, x[rows], g),
                 )
+
+            top = end_rows(slice(0, 2 * SUB), slice(0, 3 * SUB), slice(0, 2 * SUB))
+            bot = end_rows(slice(nrow, next_), slice(nrow - SUB, next_), slice(SUB, 3 * SUB))
+            w_mid = load(ar, g, mid_m)
+            lane_mid = lane_of(nrow - 2 * SUB)
+            hl = pltpu.roll(x[mid], LANES // 2 - 1 - 2 * g, 1)
+            hr = pltpu.roll(x[mid], LANES - 1 - 2 * g, 1)
+            w_mid[0] = w_mid[0] - jnp.where(lane_mid == 0, fl_x[g, mid, :LANES] * hl, 0.0)
+            w_mid[-1] = w_mid[-1] - jnp.where(
+                lane_mid == LANES - 1, fr_x[g, mid, ncol - LANES:] * hr, 0.0
+            )
+            w = [jnp.concatenate(parts, axis=0) for parts in zip(top, w_mid, bot)]
+            v = load(r_x, g, own)
             w_own = [t[own] for t in w]
             wx = halo_ar[5]
             wl, wr = left_of(w_own, wx, g), right_of(w_own, wx, g)
@@ -418,7 +475,7 @@
                 )
                 ar[g, :, sl] = c
                 aar[g, :, sl] = t
-                r = v[k][own]
+                r = v[k]
                 for i, (p, q) in enumerate(((r, r), (r, c), (c, c), (c, t))):
                     sums[i] = sums[i] + jnp.sum(p * q, axis=0, keepdims=True)
             for i in range(4):
@@ -476,7 +533,6 @@
                 r, w = r_x[g, own, sl], ar[g, :, sl]
                 e = e_out[g, :, sl] + cr * r - ci * w
                 e_out[g, :, sl] = e
-                r_x[g, own, sl] = r - cr * w + ci * aar[g, :, sl]
                 out.append(absorbed[k] + a_x[g, own, sl] * e)
             return tuple(out)
 
@@ -484,37 +540,30 @@
         send = scatter_copies(absb, it)
         for c in send:
             c.start()
+
+        @pl.when(it + 1 < ITERS)
+        def _():
+            def trail(g, o):
+                cr = cres[pl.ds(g, 1), :]
+                ci = cimg[pl.ds(g, 1), :]
+                res = []
+                for k in range(nt):
+                    sl = slice(k * LANES, (k + 1) * LANES)
+                    r = r_x[g, own, sl] - cr * ar[g, :, sl] + ci * aar[g, :, sl]
+                    r_x[g, own, sl] = r
+                    res.append(r)
+                return pack(res, g, o)
+
+            o_r[0] = lax.fori_loop(0, ng, trail, zero_pack)
+
         mnext[it, mine] = (fixed[mine] + gathered_sum(absb, it, send)) / capac[mine]
-        give = []
-        for k in range(1, nz):
-            give.append(remote(
-                mnext.at[it, mine], mnext.at[it, mine],
-                ag_s.at[it, k], ag_v.at[it, k], {"group": lax.rem(iz + k, nz)},
-            ))
-        for c in give:
-            c.start()
-        for c in give:
-            c.wait_recv()
-        for c in give + send:
+        for c in send:
             c.wait_send()
         news = get_tiles(mnext.at[it])
         for k in range(nt):
             sl = slice(k * LANES, (k + 1) * LANES)
             dmat[:, sl] = news[k] - m_out[:, sl]
             m_out[:, sl] = news[k]
-
-        @pl.when(it + 1 < ITERS)
-        def _():
-            def feed(g, o):
-                res = []
-                for k in range(nt):
-                    sl = slice(k * LANES, (k + 1) * LANES)
-                    r = r_x[g, own, sl] + a_x[g, own, sl] * wts[g] * dmat[:, sl]
-                    r_x[g, own, sl] = r
-                    res.append(r)
-                return pack(res, g, o)
-
-            o_r[0] = lax.fori_loop(0, ng, feed, zero_pack)
 
     for c in emit:
         c.wait_send()
@@ -538,10 +587,10 @@
         + [vm(*inner), vm(*inner)]
         + [vm(2, *packed), vm(2, *around), vm(2, *around)]
         + [vm(1, *packed), vm(1, *around), vm(1, *around)] * 2
-        + [vm(*around), vm(6, *packed), vm(LANES, LANES), vm(ITERS, plane, SUB, LANES)]
+        + [vm(*packed), vm(*around), vm(6, *packed), vm(LANES, LANES), vm(ITERS, plane, SUB, LANES)]
         + [vm(ng, LANES), vm(ng, LANES)]
         + [vm(*packed), vm(npol, *packed), vm(tiles, SUB, LANES), vm(tiles, SUB, LANES)]
-        + [vm(ITERS + 1, nz, tiles // nz, SUB, LANES), vm(ITERS, tiles, SUB, LANES)]
+        + [vm(ITERS + 1, nz, tiles, SUB, LANES), vm(ITERS, tiles, SUB, LANES)]
         + [vm(tiles, SUB, LANES), vm(tiles, SUB, LANES), vm(nrow, ncol)]
         + [dma(4, 2), dma(4, 2), dma(3, 2), dma(3, 2), dma(2, 4), dma(2, 4)]
         + [dma(plane), dma(ITERS, plane), dma(ITERS + 1, nz), dma(ITERS + 1, nz)]

time: 86.5 us -> 77.2 us (0.89)
  Pallas kernels: 79 us -> 69.7 us
    pallas_call x1, Pallas kernels: 79 us -> 69.7 us  [per_device(): pl.pallas_call(functools.partial(kernel, nr, npol, nz), out_shape=[jax.Sh...]
where the time goes in v2:
time: 77.2 us; the launch traced here: 76.9 us
  Pallas kernels  69.7 us (90%)
  local copies, waits for them, and re-layouts  6.5 us (8%)
    pallas_call x1, Pallas kernels, per_device(): pl.pallas_call(functools.partial(kernel, nr, npol, nz), out_shape=[jax.Sh...  69.7 us
    unnamed x15, local copies, waits for them, and re-layouts  6.5 us

profile of v2, /device:TPU:0, one launch (start us, length us, event | category | flops | bytes accessed | tf_op | source)
XLA Modules:
  0.0 76.9 jit_solution(17741933867098474358)
XLA Ops:
  0.6 0.0 copy-start.5
  0.6 0.0 copy-start.4
  0.7 0.6 copy-done.5
  1.3 0.0 copy-done.4
  1.3 0.0 copy-start
  1.3 1.1 %copy-done = f32[16,48,256]{2,1,0:T(8,128)S(1)} copy-done((f32[16,48,256]{2,1,0:T(8,128)S(1)}, f32[16,48,256]{2,1,0:T(8,128)}, u32[]{:S(2)}) %copy-start) | copy-done | bytes 786456
  2.4 0.0 copy-start.1
  2.4 1.0 %copy-done.1 = bf16[16,48,256]{2,1,0:T(8,128)(2,1)S(1)} copy-done((bf16[16,48,256]{2,1,0:T(8,128)(2,1)S(1)}, bf16[16,48,256]{2,1,0:T(8,128)(2,1)}, u32[]{:S(2)}) %copy-start.1) | copy-done | bytes 393240
  3.4 0.0 copy-start.2
  3.4 0.8 %copy-done.2 = f32[48,256]{1,0:T(8,128)S(1)} copy-done((f32[48,256]{1,0:T(8,128)S(1)}, f32[48,256]{1,0:T(8,128)}, u32[]{:S(2)}) %copy-start.2) | copy-done | bytes 49176
  4.2 0.0 copy-start.3
  4.2 0.8 %copy-done.3 = f32[48,256]{1,0:T(8,128)S(1)} copy-done((f32[48,256]{1,0:T(8,128)S(1)}, f32[48,256]{1,0:T(8,128)}, u32[]{:S(2)}) %copy-start.3) | copy-done | bytes 49176
  5.0 69.7 %shard_map.85 = (f32[16,48,256]{2,1,0:T(8,128)S(1)}, f32[48,256]{1,0:T(8,128)S(1)}, f32[48,256]{1,0:T(8,128)S(1)}) custom-call(f32[48,256]{1,0:T(8,128)S(1)} %copy-done.2, bf16[16,48,256]{2,1,0:T(8,128)(2,1)S(1)} %copy-done.1, f32[16,48,256]{2,1,0:T(8,128)S(1)} %copy-done, f32[48,256]{1,0:T(8,128)S(1)} %copy-done.3, f32[16]{0:T(128)S(1)} %copy-done.4, ...), custom_call_target="tpu_custom_call" | custom-call | tf_op jit(solution)/shard_map/pallas_call | solution.py:600
  74.8 0.9 %copy.12 = f32[16,48,256]{2,1,0:T(8,128)} copy(f32[16,48,256]{2,1,0:T(8,128)S(1)} %get-tuple-element.6) | data formatting | bytes 1572864
  75.6 0.6 copy.13
  76.3 0.6 copy.14
Async XLA Ops:
  0.6 0.7 copy-start.5
  0.6 0.7 copy-start.4
  1.3 1.1 %copy-start = (f32[16,48,256]{2,1,0:T(8,128)S(1)}, f32[16,48,256]{2,1,0:T(8,128)}, u32[]{:S(2)}) copy-start(f32[16,48,256]{2,1,0:T(8,128)} %rad.1) | copy-start | bytes 2359300
  2.4 1.0 %copy-start.1 = (bf16[16,48,256]{2,1,0:T(8,128)(2,1)S(1)}, bf16[16,48,256]{2,1,0:T(8,128)(2,1)}, u32[]{:S(2)}) copy-start(bf16[16,48,256]{2,1,0:T(8,128)(2,1)} %opac.1) | copy-start | bytes 1179652
  3.4 0.8 %copy-start.2 = (f32[48,256]{1,0:T(8,128)S(1)}, f32[48,256]{1,0:T(8,128)}, u32[]{:S(2)}) copy-start(f32[48,256]{1,0:T(8,128)} %dens.1) | copy-start | bytes 147460
  4.2 0.8 %copy-start.3 = (f32[48,256]{1,0:T(8,128)S(1)}, f32[48,256]{1,0:T(8,128)}, u32[]{:S(2)}) copy-start(f32[48,256]{1,0:T(8,128)} %mat0.1) | copy-start | bytes 147460

commit v3 on v2

--- a/solution.py
+++ b/solution.py
@@ -217,7 +217,7 @@
         em = tuple(em[k] + aw[k] for k in range(nt))
         return pack(load(rad, g, slice(None)), g, oe), pack(a, g, oa), pack(aw, g, ow), em
 
-    oe, oa, ow, em = lax.fori_loop(0, ng, first, (zero_pack, zero_pack, zero_pack, zero_tiles))
+    oe, oa, ow, em = lax.fori_loop(0, ng, first, (zero_pack, zero_pack, zero_pack, zero_tiles), unroll=2)
     o_aw[...] = ow
     o_ea[0] = oe
     o_ea[1] = oa
@@ -276,7 +276,7 @@
             d_x[g, own, k * LANES:(k + 1) * LANES] = d[k]
         return pack(d, g, od)
 
-    o_d[0] = lax.fori_loop(0, ng, second, zero_pack)
+    o_d[0] = lax.fori_loop(0, ng, second, zero_pack, unroll=2)
     dd = slab_copies(d_x, SUB, nrow, d_x, 2) + pol_copies(o_d, hl_d, hr_d, 1) + diag_copies(
         o_d, hl_d, hr_d, 0
     )
@@ -358,7 +358,7 @@
             e_out[g, :, sl] = c
         return pack(res, g, o)
 
-    o_r[0] = lax.fori_loop(0, ng, third, zero_pack)
+    o_r[0] = lax.fori_loop(0, ng, third, zero_pack, unroll=2)
     m_out[...] = mat0[...]
     dmat[...] = mat0[...]
 
@@ -380,7 +380,7 @@
         slabs = slab_copies(r_x, SUB, nrow, r_x, 3)
         start(sides)
 
-        @pl.loop(0, ng)
+        @pl.loop(0, ng, unroll=2)
         def _(g):
             for base in (0, nrow - SUB):
                 rows_x, rows_m = slice(SUB + base, 2 * SUB + base), slice(base, base + SUB)
@@ -404,7 +404,7 @@
                 )
             return out
 
-        @pl.loop(0, ng)
+        @pl.loop(0, ng, unroll=2)
         def _(g):
             v, full = [], []
             for k in range(nt):
@@ -435,7 +435,7 @@
             - halo_ar[3] * below(x_r)[own]
         )
 
-        @pl.loop(0, ng)
+        @pl.loop(0, ng, unroll=2)
         def _(g):
             x = halo_x[...]
 
@@ -492,18 +492,19 @@
                 gram.at[it, me], gram.at[it, me], gram_s.at[k], gram_v.at[it, k], where
             )
 
-        @pl.loop(1, plane)
+        @pl.loop(1, plane, unroll=min(plane - 1, 7))
         def _(k):
             gram_copy(k).start()
 
-        @pl.loop(1, plane)
+        @pl.loop(1, plane, unroll=min(plane - 1, 7))
         def _(k):
             c = gram_copy(k)
             c.wait_recv()
             c.wait_send()
 
         total = lax.fori_loop(
-            0, plane, lambda k, s: s + gram[it, k], jnp.zeros((SUB, LANES), jnp.float32)
+            0, plane, lambda k, s: s + gram[it, k], jnp.zeros((SUB, LANES), jnp.float32),
+            unroll=min(plane, 8),
         )
         spread = jnp.sum(jnp.where(pick, total[0:1], 0.0), axis=1, keepdims=True)
         norm_first = spread[0:ng]
@@ -536,7 +537,7 @@
                 out.append(absorbed[k] + a_x[g, own, sl] * e)
             return tuple(out)
 
-        put_tiles(absb, lax.fori_loop(0, ng, update, zero_tiles))
+        put_tiles(absb, lax.fori_loop(0, ng, update, zero_tiles, unroll=2))
         send = scatter_copies(absb, it)
         for c in send:
             c.start()
@@ -554,7 +555,7 @@
                     res.append(r)
                 return pack(res, g, o)
 
-            o_r[0] = lax.fori_loop(0, ng, trail, zero_pack)
+            o_r[0] = lax.fori_loop(0, ng, trail, zero_pack, unroll=2)
 
         mnext[it, mine] = (fixed[mine] + gathered_sum(absb, it, send)) / capac[mine]
         for c in send:

time: 77.2 us -> 72.2 us (0.935)
  Pallas kernels: 69.7 us -> 64.7 us
    pallas_call x1, Pallas kernels: 69.7 us -> 64.7 us  [per_device(): pl.pallas_call(functools.partial(kernel, nr, npol, nz), out_shape=[jax.Sh...]
where the time goes in v3:
time: 72.2 us; the launch traced here: 71.9 us
  Pallas kernels  64.7 us (90%)
  local copies, waits for them, and re-layouts  6.5 us (9%)
    pallas_call x1, Pallas kernels, per_device(): pl.pallas_call(functools.partial(kernel, nr, npol, nz), out_shape=[jax.Sh...  64.7 us
    unnamed x15, local copies, waits for them, and re-layouts  6.5 us

profile of v3, /device:TPU:0, one launch (start us, length us, event | category | flops | bytes accessed | tf_op | source)
XLA Modules:
  0.0 71.9 jit_solution(5751982239527121349)
XLA Ops:
  0.6 0.0 copy-start.5
  0.6 0.0 copy-start.4
  0.7 0.6 copy-done.5
  1.3 0.0 copy-done.4
  1.3 0.0 copy-start
  1.3 1.1 %copy-done = f32[16,48,256]{2,1,0:T(8,128)S(1)} copy-done((f32[16,48,256]{2,1,0:T(8,128)S(1)}, f32[16,48,256]{2,1,0:T(8,128)}, u32[]{:S(2)}) %copy-start) | copy-done | bytes 786456
  2.4 0.0 copy-start.1
  2.4 1.0 %copy-done.1 = bf16[16,48,256]{2,1,0:T(8,128)(2,1)S(1)} copy-done((bf16[16,48,256]{2,1,0:T(8,128)(2,1)S(1)}, bf16[16,48,256]{2,1,0:T(8,128)(2,1)}, u32[]{:S(2)}) %copy-start.1) | copy-done | bytes 393240
  3.4 0.0 copy-start.2
  3.4 0.8 %copy-done.2 = f32[48,256]{1,0:T(8,128)S(1)} copy-done((f32[48,256]{1,0:T(8,128)S(1)}, f32[48,256]{1,0:T(8,128)}, u32[]{:S(2)}) %copy-start.2) | copy-done | bytes 49176
  4.2 0.0 copy-start.3
  4.2 0.8 %copy-done.3 = f32[48,256]{1,0:T(8,128)S(1)} copy-done((f32[48,256]{1,0:T(8,128)S(1)}, f32[48,256]{1,0:T(8,128)}, u32[]{:S(2)}) %copy-start.3) | copy-done | bytes 49176
  5.0 64.7 %shard_map.85 = (f32[16,48,256]{2,1,0:T(8,128)S(1)}, f32[48,256]{1,0:T(8,128)S(1)}, f32[48,256]{1,0:T(8,128)S(1)}) custom-call(f32[48,256]{1,0:T(8,128)S(1)} %copy-done.2, bf16[16,48,256]{2,1,0:T(8,128)(2,1)S(1)} %copy-done.1, f32[16,48,256]{2,1,0:T(8,128)S(1)} %copy-done, f32[48,256]{1,0:T(8,128)S(1)} %copy-done.3, f32[16]{0:T(128)S(1)} %copy-done.4, ...), custom_call_target="tpu_custom_call" | custom-call | tf_op jit(solution)/shard_map/pallas_call | solution.py:601
  69.8 0.9 %copy.12 = f32[16,48,256]{2,1,0:T(8,128)} copy(f32[16,48,256]{2,1,0:T(8,128)S(1)} %get-tuple-element.6) | data formatting | bytes 1572864
  70.7 0.6 copy.13
  71.3 0.6 copy.14
Async XLA Ops:
  0.6 0.7 copy-start.5
  0.6 0.7 copy-start.4
  1.3 1.1 %copy-start = (f32[16,48,256]{2,1,0:T(8,128)S(1)}, f32[16,48,256]{2,1,0:T(8,128)}, u32[]{:S(2)}) copy-start(f32[16,48,256]{2,1,0:T(8,128)} %rad.1) | copy-start | bytes 2359300
  2.4 1.0 %copy-start.1 = (bf16[16,48,256]{2,1,0:T(8,128)(2,1)S(1)}, bf16[16,48,256]{2,1,0:T(8,128)(2,1)}, u32[]{:S(2)}) copy-start(bf16[16,48,256]{2,1,0:T(8,128)(2,1)} %opac.1) | copy-start | bytes 1179652
  3.4 0.8 %copy-start.2 = (f32[48,256]{1,0:T(8,128)S(1)}, f32[48,256]{1,0:T(8,128)}, u32[]{:S(2)}) copy-start(f32[48,256]{1,0:T(8,128)} %dens.1) | copy-start | bytes 147460
  4.2 0.8 %copy-start.3 = (f32[48,256]{1,0:T(8,128)S(1)}, f32[48,256]{1,0:T(8,128)}, u32[]{:S(2)}) copy-start(f32[48,256]{1,0:T(8,128)} %mat0.1) | copy-start | bytes 147460
